TPU v7x, 256 devices: a whole 4x4x8 slice. The times are simulated.
256 devices in a mesh: tok: 64 (over z, x, core), hv: 4 (over y).
Axes of the slice: x: 4, y: 4, z: 8, core: 2. Of those that a mesh axis runs over, the one named last changes fastest.
Arguments:
- tokens: bfloat16 [16384, 2048], P(('tok', 'hv')), may hold values from -6 to 6
- prompt_lengths: int32 [33], replicated, may hold values from 1 to 10922, 16384 in all
- query_weight: bfloat16 [2048, 1024], P(None, 'hv'), may hold values from -0.125 to 0.125
- key_weight: bfloat16 [2048, 1024], P(None, 'hv'), may hold values from -0.125 to 0.125
- value_weight: bfloat16 [2048, 2048], P(None, 'hv'), may hold values from -0.125 to 0.125
- query_conv: bfloat16 [4, 1024], P(None, 'hv'), may hold values from -3 to 3
- key_conv: bfloat16 [4, 1024], P(None, 'hv'), may hold values from -3 to 3
- value_conv: bfloat16 [4, 2048], P(None, 'hv'), may hold values from -3 to 3
- decay_down: bfloat16 [2048, 16], replicated, may hold values from -0.125 to 0.125
- decay_up: bfloat16 [16, 1024], P(None, 'hv'), may hold values from -3 to 3
- decay_bias: float32 [1024], P('hv')
- gate_weight: bfloat16 [2048, 2048], P(None, 'hv'), may hold values from -0.125 to 0.125
- norm_gain: float32 [512], replicated, may hold values from 0.1 to 1.9
- out_weight: bfloat16 [2048, 2048], P('hv'), may hold values from -0.125 to 0.125
Outputs:
- mixed: bfloat16 [16384, 2048], P(('tok', 'hv'))
- segment_states: float32 [64, 4, 256, 512], P('tok', 'hv')
- conv_edges: bfloat16 [64, 3, 4, 1024], P('tok', None, 'hv')
Inputs may be any that keep to these rules, and one draw needn't show every extreme that they name: `prompt_lengths`: the rows of 33 prompts that fill all 16384 packed rows; exactly one prompt has 10922 rows.
All inputs are finite; a program needn't handle non-finite values.
Results may differ from a plain program's by a relative error of at most 0.022.
Values may be sent and summed in bfloat16 or wider, within the bound.
A program may use at most 128 MiB of HBM per device.

v0:
```python
import jax
import jax.numpy as jnp
from jax import lax
from jax.sharding import PartitionSpec as P

SPAN = 64
HIGHEST_PRECISION = lax.Precision.HIGHEST


def shifted(value, axis, steps):
    count = lax.axis_size(axis)
    initial, last = (max(0, -steps), min(count, count - steps))
    return lax.ppermute(value, axis, [(source, source + steps) for source in range(initial, last)])


def carried_in(part, axis, combine, identity):
    place = lax.axis_index(axis)
    gathered = jax.tree.map(lambda a: lax.all_gather(a, axis), part)
    state = jax.tree.map(lambda a, e: jnp.zeros_like(a) + jnp.asarray(e, a.dtype), part, identity)

    def one(lap, state):
        return combine(
            state, jax.tree.map(lambda a: lax.dynamic_index_in_dim(a, lap, 0, False), gathered)
        )

    return lax.fori_loop(0, place, one, state)


def prompt_marks(positions, offsets):
    before = offsets[None, :] <= positions[:, None]
    prompt_first = jnp.max(jnp.where(before, offsets[None, :], 0), axis=1)
    return (prompt_first, (prompt_first == positions).astype(jnp.float32))


def short_conv(raw_rows, before_rows, weight, positions, prompt_first):
    tap_count = weight.shape[0]
    extended = jnp.concatenate([before_rows, raw_rows], axis=0)
    summed = jnp.zeros(raw_rows.shape, jnp.float32)
    for tap_index in range(tap_count):
        lag_rows = tap_count - 1 - tap_index
        inside_prompt = (positions - lag_rows >= prompt_first).astype(jnp.float32)
        window = lax.slice_in_dim(extended, tap_index, tap_index + raw_rows.shape[0], axis=0)
        summed = (
            summed
            + weight[tap_index].astype(jnp.float32)[None, :]
            * window.astype(jnp.float32)
            * inside_prompt[:, None]
        )
    return jax.nn.silu(summed).astype(jnp.bfloat16)


def span_parts(head_keys, head_values, decays, starts):
    cumulative = jnp.cumsum(decays, axis=0)
    groups = jnp.cumsum(starts)
    intact = (groups == 0.0).astype(jnp.float32)
    final_log = cumulative[-1]
    in_tail = (groups == groups[-1]).astype(jnp.float32)
    weighted = (
        head_keys.astype(jnp.float32) * jnp.exp(final_log[None, :] - cumulative) * in_tail[:, None]
    ).astype(jnp.bfloat16)
    update = lax.dot_general(
        weighted, head_values, (((0,), (0,)), ((), ())), preferred_element_type=jnp.float32
    )
    step_decay = jnp.exp(final_log) * intact[-1]
    return (cumulative, groups, intact, update, step_decay)


def state_step(carried, pieces):
    memory, product = carried
    head_keys, head_values, decays, starts = pieces
    _, _, _, update, step_decay = span_parts(head_keys, head_values, decays, starts)
    return ((step_decay[:, None] * memory + update, product * step_decay), None)


def span_step(carried, pieces):
    memory, product = carried
    queries, head_keys, head_values, decays, starts = pieces
    cumulative, groups, intact, update, step_decay = span_parts(
        head_keys, head_values, decays, starts
    )
    index_rows = jnp.arange(queries.shape[0])
    allowed = (groups[:, None] == groups[None, :]) & (index_rows[:, None] >= index_rows[None, :])
    lifted = queries.astype(jnp.float32) * jnp.exp(cumulative)
    lowered = (head_keys.astype(jnp.float32) * jnp.exp(-cumulative)).astype(jnp.bfloat16)
    raw_scores = lax.dot_general(
        lifted.astype(jnp.bfloat16),
        lowered,
        (((1,), (1,)), ((), ())),
        preferred_element_type=jnp.float32,
    )
    scores = jnp.where(allowed, raw_scores, 0.0).astype(jnp.bfloat16)
    inside = jnp.dot(scores, head_values, preferred_element_type=jnp.float32)
    outside = jnp.dot(lifted * intact[:, None], memory, precision=HIGHEST_PRECISION)
    reaches = product[None, :] * jnp.exp(cumulative) * intact[:, None]
    return (
        (step_decay[:, None] * memory + update, product * step_decay),
        (inside + outside, reaches),
    )


def blocked(array_in):
    return array_in.reshape((array_in.shape[0] // SPAN, SPAN) + array_in.shape[1:])


def sweep(queries, head_keys, head_values, decays, starts, memory):
    initial = (memory, jnp.ones((decays.shape[1],), jnp.float32))
    (closing, product), (outputs, reaches) = lax.scan(
        span_step,
        initial,
        (
            blocked(queries),
            blocked(head_keys),
            blocked(head_values),
            blocked(decays),
            blocked(starts),
        ),
    )
    row_count = queries.shape[0]
    return (
        outputs.reshape((row_count, head_values.shape[1])),
        reaches.reshape((row_count, decays.shape[1])),
        closing,
        product,
    )


def combine(earlier, following):
    return (earlier[0] * following[0], following[0][:, None] * earlier[1] + following[1])


def shards(
    tokens,
    prompt_lengths,
    query_weight,
    key_weight,
    value_weight,
    query_conv,
    key_conv,
    value_conv,
    decay_down,
    decay_up,
    decay_bias,
    gate_weight,
    norm_gain,
    out_weight,
):
    gathered = lax.all_gather(tokens, "hv", axis=0, tiled=True)

    def project(weight):
        return jnp.dot(gathered, weight, preferred_element_type=jnp.float32).astype(jnp.bfloat16)

    raw_query = project(query_weight)
    raw_key = project(key_weight)
    raw_value = project(value_weight)
    gate_values = project(gate_weight)
    low_rank = project(decay_down)
    row_count = raw_query.shape[0]
    key_width = raw_query.shape[1]
    value_width = raw_value.shape[1]
    positions = lax.axis_index("tok") * row_count + jnp.arange(row_count, dtype=jnp.int32)
    offsets = jnp.cumsum(prompt_lengths) - prompt_lengths
    prompt_first, starts = prompt_marks(positions, offsets)
    rim_rows = query_conv.shape[0] - 1
    joined = jnp.concatenate([raw_query, raw_key, raw_value], axis=1)
    before_rows = shifted(joined[row_count - rim_rows :], "tok", 1)
    conv_query = short_conv(
        raw_query, before_rows[:, :key_width], query_conv, positions, prompt_first
    )
    conv_key = short_conv(
        raw_key, before_rows[:, key_width : 2 * key_width], key_conv, positions, prompt_first
    )
    conv_value = short_conv(
        raw_value, before_rows[:, 2 * key_width :], value_conv, positions, prompt_first
    )
    decays = (
        jax.nn.log_sigmoid(
            jnp.dot(low_rank, decay_up, preferred_element_type=jnp.float32) + decay_bias
        )
        / 16.0
    )
    empty_memory = jnp.zeros((key_width, value_width), jnp.float32)
    ones_decay = jnp.ones((key_width,), jnp.float32)
    (local_memory, local_decay), _ = lax.scan(
        state_step,
        (empty_memory, ones_decay),
        (blocked(conv_key), blocked(conv_value), blocked(decays), blocked(starts)),
    )
    entering_decay, entering = carried_in(
        (local_decay, local_memory), "tok", combine, (ones_decay, empty_memory)
    )
    heads_out, _, closing, _ = sweep(conv_query, conv_key, conv_value, decays, starts, entering)
    gate_float = gate_values.astype(jnp.float32)
    rescale = lax.rsqrt(jnp.mean(heads_out * heads_out, axis=1, keepdims=True) + 1e-05)
    gated_out = (
        heads_out * rescale * norm_gain[None, :] * gate_float * jax.nn.sigmoid(gate_float)
    ).astype(jnp.bfloat16)
    mixed = lax.psum_scatter(
        jnp.dot(gated_out, out_weight, preferred_element_type=jnp.float32).astype(jnp.bfloat16),
        "hv",
        scatter_dimension=0,
        tiled=True,
    )
    segment_states = closing[None, None]
    in_prompt = positions[row_count - rim_rows :] >= prompt_first[row_count - 1]
    tail_rows = joined[row_count - rim_rows :]
    conv_edges = jnp.where(in_prompt[:, None], tail_rows, jnp.zeros_like(tail_rows))
    conv_edges = conv_edges.reshape((1, rim_rows, 1, joined.shape[1]))
    return (mixed, segment_states, conv_edges)


def solution(mesh):
    in_specs = (
        P(("tok", "hv"), None),
        P(),
        P(None, "hv"),
        P(None, "hv"),
        P(None, "hv"),
        P(None, "hv"),
        P(None, "hv"),
        P(None, "hv"),
        P(),
        P(None, "hv"),
        P("hv"),
        P(None, "hv"),
        P(),
        P("hv", None),
    )
    out_specs = (P(("tok", "hv"), None), P("tok", "hv", None, None), P("tok", None, "hv", None))
    return jax.shard_map(shards, mesh=mesh, in_specs=in_specs, out_specs=out_specs, check_vma=False)
```

profile of v0, /device:TPU:2, one launch (start us, length us, event | category | flops | bytes accessed | tf_op | source)
XLA Modules:
  0.0 348.6 jit_solution(8499154411287329581)
XLA Ops:
  11.6 1.4 slice_convert_fusion.11
  13.8 25.5 %all-gather.6.cloned.1.call-done = bf16[256,2048]{1,0:T(8,128)(2,1)} async-done(((bf16[64,2048]{1,0:T(8,128)(2,1)}), bf16[256,2048]{1,0:T(8,128)(2,1)}) %all-gather.6.cloned.1.call-update) | async-done | bytes 1048592 | tf_op jit(solution)/shard_map/all_gather | solution.py:147
  39.4 2.8 convolution_convert_fusion.2
  43.8 1.9 collective-permute-start
  45.7 2.0 fusion.69
  48.7 2.0 multiply_convert_fusion
  52.2 13.0 %while.39 = (s32[]{:T(128)}, f32[256,512]{1,0:T(8,128)S(1)}, f32[256]{0:T(256)S(1)}, f32[4,64,256]{2,1,0:T(8,128)S(1)}, f32[4,64]{1,0:T(4,128)}, /*index=5*/bf16...) while((s32[]{:T(128)}, f32[256,512]{1,0:T(8,128)S(1)}, ...), condition=%wide.region_5.6_spmd.clone, body=%wide.region_2.5_spmd.clone.sunk | while | flops 18289476 | bytes 1486494 | solution.py:183
  67.0 45.3 %all-gather.2 = f32[64,1,256]{2,1,0:T(1,128)S(1)} all-gather(f32[1,1,256]{2,1,0:T(1,128)S(1)} %bitcast.205), channel_id=2, replica_groups=mesh['tok'=64,'hv'=4] {'tok'}, dimensions={0}, use_global_device_ids=true | all-gather | bytes 66560 | tf_op jit(solution)/shard_map/all_gather | solution.py:18
  112.3 1.7 multiply_convert_fusion.1
  114.0 94.5 %all-gather.8.cloned.1.call-done = f32[16384,512]{1,0:T(8,128)} async-done(((f32[256,512]{1,0:T(8,128)}), f32[16384,512]{1,0:T(8,128)}) %all-gather.8.cloned.1.call-update) | async-done | bytes 33554448 | tf_op jit(solution)/shard_map/all_gather | solution.py:18
  208.5 2.5 while.37
  208.6 1.2 bitcast_add_fusion.2
  209.8 1.2 bitcast_add_fusion.2
  211.0 27.2 %while.38 = (s32[]{:T(128)}, f32[256,512]{1,0:T(8,128)S(1)}, f32[4,64,512]{2,1,0:T(8,128)}, f32[4,64,256]{2,1,0:T(8,128)S(1)}, f32[4,64]{1,0:T(4,128)}, /*index=...) while((s32[]{:T(128)}, f32[256,512]{1,0:T(8,128)S(1)}, ...), condition=%wide.region_11.12_spmd, body=%wide.region_8.11_spmd.sunk | while | flops 125329856 | bytes 2767001 | solution.py:107
  212.1 1.0 fusion.111
  214.3 1.9 fusion.112
  218.9 1.0 fusion.111
  221.1 1.9 fusion.112
  227.9 1.9 fusion.112
  234.7 1.9 fusion.112
  238.2 1.3 multiply_reduce_fusion
  239.7 2.8 fusion.65
  242.5 1.7 convolution_convert_fusion
  244.2 97.8 %reduce-scatter.2.cloned.1.call-done = bf16[64,2048]{1,0:T(8,128)(2,1)} async-done(((bf16[256,2048]{1,0:T(8,128)(2,1)}), bf16[64,2048]{1,0:T(8,128)(2,1)}) %reduce-scatter.2.cloned.1.call-update) | async-done | bytes 262160 | tf_op jit(solution)/shard_map/reduce_scatter | solution.py:197
  (151 shorter events, 38.8 us)
Async XLA Ops:
  7.2 235.3 %copy-start = (bf16[512,2048]{1,0:T(8,128)(2,1)S(1)}, bf16[512,2048]{1,0:T(8,128)(2,1)}, u32[]{:S(2)}) copy-start(bf16[512,2048]{1,0:T(8,128)(2,1)} %param.33) | copy-start | bytes 6291460
  7.2 32.2 %all-gather.6.cloned.1.call-start = ((), (), s32[]{:S(2)}) async-start(), calls=%async_computation.1 | async-start | bytes 1310720 | tf_op jit(solution)/shard_map/all_gather | solution.py:147
  7.9 200.5 %all-gather.8.cloned.1.call-start = ((), (), s32[]{:S(2)}) async-start(), calls=%async_computation.3 | async-start | bytes 34078720 | tf_op jit(solution)/shard_map/all_gather | solution.py:18
  11.6 37.2 %copy-start.8 = (f32[256]{0:T(256)}, f32[256]{0:T(256)S(1)}, u32[]{:S(2)}) copy-start(f32[256]{0:T(256)S(1)} %get-tuple-element.220) | copy-start | bytes 3076
  11.6 39.7 %copy-start.7 = (f32[256]{0:T(256)}, f32[256]{0:T(256)S(1)}, u32[]{:S(2)}) copy-start(f32[256]{0:T(256)S(1)} %get-tuple-element.219) | copy-start | bytes 3076
  39.4 2.8 copy-start.3
  39.4 2.8 copy-start.5
  39.4 3.3 copy-start.6
  42.1 0.9 copy-start.4
  42.2 3.5 %copy-start.9 = (bf16[2048,16]{0,1:T(8,128)(2,1)S(1)}, bf16[2048,16]{0,1:T(8,128)(2,1)}, u32[]{:S(2)}) copy-start(bf16[2048,16]{0,1:T(8,128)(2,1)} %param.28) | copy-start | bytes 196612
  42.2 3.5 %copy-start.10 = (bf16[16,256]{1,0:T(8,128)(2,1)S(1)}, bf16[16,256]{1,0:T(8,128)(2,1)}, u32[]{:S(2)}) copy-start(bf16[16,256]{1,0:T(8,128)(2,1)} %param.29) | copy-start | bytes 24580
  42.2 3.5 %copy-start.12 = (f32[256]{0:T(256)S(1)}, f32[256]{0:T(256)}, u32[]{:S(2)}) copy-start(f32[256]{0:T(256)} %param.30) | copy-start | bytes 3076
  43.8 5.0 %collective-permute-start = (bf16[3,1024]{1,0:T(4,128)(2,1)S(1)}, bf16[3,1024]{1,0:T(4,128)(2,1)S(1)}, u32[]{:S(2)}, u32[]{:S(2)}) collective-permute-start(bf16[3,1024]{1,0:T(4,128)(2,1)S(1)} %get-tuple-element.200), channel_id=1, source_target_pairs={{0,4},{4,8},{8,12},{12,16},{16,20},{20,24},{24,28},{28,32},{32,36}... | collective-permute-start | bytes 18440 | tf_op jit(solution)/shard_map/ppermute | solution.py:13
  65.3 0.8 copy-start.2
  66.1 275.9 %reduce-scatter.2.cloned.1.call-start = ((), (), s32[]{:S(2)}) async-start(), calls=%async_computation.2 | async-start | bytes 1310720 | tf_op jit(solution)/shard_map/reduce_scatter | solution.py:197
  211.0 28.7 %copy-start.11 = (f32[512]{0:T(512)S(1)}, f32[512]{0:T(512)}, u32[]{:S(2)}) copy-start(f32[512]{0:T(512)} %param.32) | copy-start | bytes 6148
  238.2 4.2 %copy-start.1 = (f32[256,512]{1,0:T(8,128)}, f32[256,512]{1,0:T(8,128)S(1)}, u32[]{:S(2)}) copy-start(f32[256,512]{1,0:T(8,128)S(1)} %get-tuple-element.132) | copy-start | bytes 1572868
Sparse Core Ops, SparseCore 0:
  9.8 29.4 all-gather.5
  66.2 142.1 all-gather.7
  244.3 97.6 reduce-scatter.1
where the time goes:
time: 353 us; the launch traced here: 349 us
  waiting for transfers between devices  220 us (62%)
  blocking collectives  45.3 us (13%)
  matrix products  24.7 us (7%)
  other arithmetic  24.5 us (7%)
  local copies, waits for them, and re-layouts  15.4 us (4%)
  between operations  14 us (4%)
    reduce_scatter x1, waiting for transfers between devices, shards(): lax.psum_scatter(jnp.dot(gated_out, out_weight, preferred_element_type=jn...  97.8 us
    all_gather x1, waiting for transfers between devices, carried_in(): gathered = jax.tree.map(lambda a: lax.all_gather(a, axis), part)  94.5 us
    all_gather x1, blocking collectives, carried_in(): gathered = jax.tree.map(lambda a: lax.all_gather(a, axis), part)  45.3 us
    all_gather x1, waiting for transfers between devices, shards(): gathered = lax.all_gather(tokens, 'hv', axis=0, tiled=True)  25.5 us
    dot_general x4, matrix products, span_step(): jnp.dot(lifted * intact[:, None], memory, precision=HIGHEST_PRECISION)  7.52 us
  transfers between devices with their start and end apart: 4, of which 4 were waited for; matrix products, arithmetic and copies ran while one was open for 3% of the time, Pallas kernels for 0%

commit v1 on v0

--- a/solution.py
+++ b/solution.py
@@ -144,7 +144,12 @@
     norm_gain,
     out_weight,
 ):
-    gathered = lax.all_gather(tokens, "hv", axis=0, tiled=True)
+    ring = [tokens]
+    for hop in range(3):
+        ring.append(lax.ppermute(ring[-1], "hv", [(dev, (dev + 1) % 4) for dev in range(4)]))
+    gathered = jnp.roll(
+        jnp.concatenate(ring[::-1], axis=0), (lax.axis_index("hv") + 1) * ring[0].shape[0], axis=0
+    )
 
     def project(weight):
         return jnp.dot(gathered, weight, preferred_element_type=jnp.float32).astype(jnp.bfloat16)

time: 353 us -> 350 us (level)
  waiting for transfers between devices: 220 us -> 210 us
  local copies, waits for them, and re-layouts: 15.4 us -> 19.9 us
    all_gather x1 -> x0, waiting for transfers between devices: 25.5 us -> none  [shards(): gathered = lax.all_gather(tokens, 'hv', axis=0, tiled=True)]
    ppermute x0 -> x3, waiting for transfers between devices: none -> 17.8 us  [shards(): lax.ppermute(ring[-1], 'hv', [(dev, (dev + 1) % 4) for dev in range(4)])]
    unnamed x27 -> x38, local copies, waits for them, and re-layouts: 0.86 us -> 4.91 us
  transfers between devices with their start and end apart: 4 -> 6, of which waited for: 4 -> 6; matrix products, arithmetic and copies ran while one was open for 3% -> 3% of each run, Pallas kernels for 0% -> 0%
where the time goes in v1:
time: 350 us; the launch traced here: 345 us
  waiting for transfers between devices  210 us (60%)
  blocking collectives  46.7 us (13%)
  other arithmetic  24.6 us (7%)
  matrix products  22.7 us (6%)
  local copies, waits for them, and re-layouts  19.9 us (6%)
  between operations  14.4 us (4%)
  starting transfers between devices  3.94 us (1%)
    reduce_scatter x1, waiting for transfers between devices, shards(): lax.psum_scatter(jnp.dot(gated_out, out_weight, preferred_element_type=jn...  97.7 us
    all_gather x1, waiting for transfers between devices, carried_in(): gathered = jax.tree.map(lambda a: lax.all_gather(a, axis), part)  93.2 us
    all_gather x1, blocking collectives, carried_in(): gathered = jax.tree.map(lambda a: lax.all_gather(a, axis), part)  46.7 us
    ppermute x3, waiting for transfers between devices, shards(): lax.ppermute(ring[-1], 'hv', [(dev, (dev + 1) % 4) for dev in range(4)])  17.8 us
    dot_general x4, matrix products, span_step(): jnp.dot(lifted * intact[:, None], memory, precision=HIGHEST_PRECISION)  7.54 us
  transfers between devices with their start and end apart: 6, of which 6 were waited for; matrix products, arithmetic and copies ran while one was open for 3% of the time, Pallas kernels for 0%

profile of v1, /device:TPU:2, one launch (start us, length us, event | category | flops | bytes accessed | tf_op | source)
XLA Modules:
  0.0 345.2 jit_solution(6937522694474735898)
XLA Ops:
  7.2 1.7 collective-permute-start
  10.7 6.2 %collective-permute-done = bf16[64,2048]{1,0:T(8,128)(2,1)S(1)} collective-permute-done((bf16[64,2048]{1,0:T(8,128)(2,1)}, bf16[64,2048]{1,0:T(8,128)(2,1)S(1)}, u32[]{:S(2)}, u32[]{:S(2)}) %collective-permute-start) | collective-permute-done | bytes 262176 | tf_op jit(solution)/shard_map/ppermute | solution.py:149
  18.3 1.4 slice_convert_fusion.11
  19.8 5.6 %collective-permute-done.1 = bf16[64,2048]{1,0:T(8,128)(2,1)S(1)} collective-permute-done((bf16[64,2048]{1,0:T(8,128)(2,1)S(1)}, bf16[64,2048]{1,0:T(8,128)(2,1)S(1)}, u32[]{:S(2)}, u32[]{:S(2)}) %collective-permute-start.1) | collective-permute-done | bytes 262176 | tf_op jit(solution)/shard_map/ppermute | solution.py:149
  26.9 6.1 %collective-permute-done.2 = bf16[64,2048]{1,0:T(8,128)(2,1)} collective-permute-done((bf16[64,2048]{1,0:T(8,128)(2,1)S(1)}, bf16[64,2048]{1,0:T(8,128)(2,1)}, u32[]{:S(2)}, u32[]{:S(2)}) %collective-permute-start.2) | collective-permute-done | bytes 262176 | tf_op jit(solution)/shard_map/ppermute | solution.py:149
  39.5 1.9 collective-permute-start.3
  41.4 2.0 fusion.77
  44.4 2.0 multiply_convert_fusion
  47.9 13.3 %while.39 = (s32[]{:T(128)}, f32[256,512]{1,0:T(8,128)S(1)}, f32[256]{0:T(256)S(1)}, f32[4,64,256]{2,1,0:T(8,128)S(1)}, f32[4,64]{1,0:T(4,128)}, /*index=5*/bf16...) while((s32[]{:T(128)}, f32[256,512]{1,0:T(8,128)S(1)}, ...), condition=%wide.region_5.6_spmd.clone, body=%wide.region_2.5_spmd.clone.sunk | while | flops 18289476 | bytes 1486494 | solution.py:188
  62.9 46.7 %all-gather.2 = f32[64,1,256]{2,1,0:T(1,128)S(1)} all-gather(f32[1,1,256]{2,1,0:T(1,128)S(1)} %bitcast.200), channel_id=2, replica_groups=mesh['tok'=64,'hv'=4] {'tok'}, dimensions={0}, use_global_device_ids=true | all-gather | bytes 66560 | tf_op jit(solution)/shard_map/all_gather | solution.py:18
  109.7 1.7 multiply_convert_fusion.1
  111.4 93.2 %all-gather.5.cloned.1.call-done = f32[16384,512]{1,0:T(8,128)} async-done(((f32[256,512]{1,0:T(8,128)}), f32[16384,512]{1,0:T(8,128)}) %all-gather.5.cloned.1.call-update) | async-done | bytes 33554448 | tf_op jit(solution)/shard_map/all_gather | solution.py:18
  204.7 2.5 while.37
  204.7 1.2 bitcast_add_fusion.2
  205.9 1.2 bitcast_add_fusion.2
  207.2 27.4 %while.38 = (s32[]{:T(128)}, f32[256,512]{1,0:T(8,128)S(1)}, f32[4,64,512]{2,1,0:T(8,128)}, f32[4,64,256]{2,1,0:T(8,128)S(1)}, f32[4,64]{1,0:T(4,128)}, /*index=...) while((s32[]{:T(128)}, f32[256,512]{1,0:T(8,128)S(1)}, ...), condition=%wide.region_11.12_spmd, body=%wide.region_8.11_spmd.sunk | while | flops 125329856 | bytes 2767001 | solution.py:107
  210.5 1.9 fusion.123
  217.4 1.9 fusion.123
  224.2 1.9 fusion.123
  231.1 1.9 fusion.123
  234.6 1.3 multiply_reduce_fusion
  236.1 2.8 fusion.71
  238.9 1.7 convolution_convert_fusion
  240.6 97.7 %reduce-scatter.2.cloned.1.call-done = bf16[64,2048]{1,0:T(8,128)(2,1)} async-done(((bf16[256,2048]{1,0:T(8,128)(2,1)}), bf16[64,2048]{1,0:T(8,128)(2,1)}) %reduce-scatter.2.cloned.1.call-update) | async-done | bytes 262160 | tf_op jit(solution)/shard_map/reduce_scatter | solution.py:202
  (166 shorter events, 45.8 us)
Async XLA Ops:
  7.2 231.7 %copy-start = (bf16[512,2048]{1,0:T(8,128)(2,1)S(1)}, bf16[512,2048]{1,0:T(8,128)(2,1)}, u32[]{:S(2)}) copy-start(bf16[512,2048]{1,0:T(8,128)(2,1)} %param.33) | copy-start | bytes 6291460
  7.2 28.8 %copy-start.7 = (bf16[64,2048]{1,0:T(8,128)(2,1)S(1)}, bf16[64,2048]{1,0:T(8,128)(2,1)}, u32[]{:S(2)}) copy-start(bf16[64,2048]{1,0:T(8,128)(2,1)} %param.20) | copy-start | bytes 786436
  7.2 197.4 %all-gather.5.cloned.1.call-start = ((), (), s32[]{:S(2)}) async-start(), calls=%async_computation.2 | async-start | bytes 34078720 | tf_op jit(solution)/shard_map/all_gather | solution.py:18
  7.2 9.6 %collective-permute-start = (bf16[64,2048]{1,0:T(8,128)(2,1)}, bf16[64,2048]{1,0:T(8,128)(2,1)S(1)}, u32[]{:S(2)}, u32[]{:S(2)}) collective-permute-start(bf16[64,2048]{1,0:T(8,128)(2,1)} %param.20), channel_id=1, source_target_pairs={{0,1},{1,2},{2,3},{3,0},{4,5},{5,6},{6,7},{7,4},{8,9},{9,10},{10,1... | collective-permute-start | bytes 786440 | tf_op jit(solution)/shard_map/ppermute | solution.py:149
  10.7 33.8 %copy-start.9 = (f32[256]{0:T(256)}, f32[256]{0:T(256)S(1)}, u32[]{:S(2)}) copy-start(f32[256]{0:T(256)S(1)} %get-tuple-element.220) | copy-start | bytes 3076
  10.7 36.3 %copy-start.8 = (f32[256]{0:T(256)}, f32[256]{0:T(256)S(1)}, u32[]{:S(2)}) copy-start(f32[256]{0:T(256)S(1)} %get-tuple-element.219) | copy-start | bytes 3076
  16.8 8.5 %collective-permute-start.1 = (bf16[64,2048]{1,0:T(8,128)(2,1)S(1)}, bf16[64,2048]{1,0:T(8,128)(2,1)S(1)}, u32[]{:S(2)}, u32[]{:S(2)}) collective-permute-start(bf16[64,2048]{1,0:T(8,128)(2,1)S(1)} %collective-permute-done), channel_id=1, source_target_pairs={{0,1},{1,2},{2,3},{3,0},{4,5},{5,6},{6,7},{7,4},{8,9},{9,10},{10,1... | collective-permute-start | bytes 786440 | tf_op jit(solution)/shard_map/ppermute | solution.py:149
  25.3 7.7 %collective-permute-start.2 = (bf16[64,2048]{1,0:T(8,128)(2,1)S(1)}, bf16[64,2048]{1,0:T(8,128)(2,1)}, u32[]{:S(2)}, u32[]{:S(2)}) collective-permute-start(bf16[64,2048]{1,0:T(8,128)(2,1)S(1)} %collective-permute-done.1), channel_id=1, source_target_pairs={{0,1},{1,2},{2,3},{3,0},{4,5},{5,6},{6,7},{7,4},{8,9},{9,10},{10,1... | collective-permute-start | bytes 786440 | tf_op jit(solution)/shard_map/ppermute | solution.py:149
  26.9 9.2 %copy-start.10 = (bf16[2048,512]{1,0:T(8,128)(2,1)S(1)}, bf16[2048,512]{1,0:T(8,128)(2,1)}, u32[]{:S(2)}) copy-start(bf16[2048,512]{1,0:T(8,128)(2,1)} %param.24) | copy-start | bytes 6291460
  36.0 1.8 copy-start.4
  36.1 2.3 copy-start.3
  36.1 2.3 copy-start.5
  37.9 0.9 copy-start.6
  37.9 3.5 %copy-start.11 = (bf16[2048,16]{0,1:T(8,128)(2,1)S(1)}, bf16[2048,16]{0,1:T(8,128)(2,1)}, u32[]{:S(2)}) copy-start(bf16[2048,16]{0,1:T(8,128)(2,1)} %param.28) | copy-start | bytes 196612
  37.9 3.5 %copy-start.12 = (bf16[16,256]{1,0:T(8,128)(2,1)S(1)}, bf16[16,256]{1,0:T(8,128)(2,1)}, u32[]{:S(2)}) copy-start(bf16[16,256]{1,0:T(8,128)(2,1)} %param.29) | copy-start | bytes 24580
  37.9 3.5 %copy-start.14 = (f32[256]{0:T(256)S(1)}, f32[256]{0:T(256)}, u32[]{:S(2)}) copy-start(f32[256]{0:T(256)} %param.30) | copy-start | bytes 3076
  39.5 5.0 %collective-permute-start.3 = (bf16[3,1024]{1,0:T(4,128)(2,1)S(1)}, bf16[3,1024]{1,0:T(4,128)(2,1)S(1)}, u32[]{:S(2)}, u32[]{:S(2)}) collective-permute-start(bf16[3,1024]{1,0:T(4,128)(2,1)S(1)} %get-tuple-element.200), channel_id=1, source_target_pairs={{0,4},{4,8},{8,12},{12,16},{16,20},{20,24},{24,28},{28,32},{32,36}... | collective-permute-start | bytes 18440 | tf_op jit(solution)/shard_map/ppermute | solution.py:13
  61.2 0.8 copy-start.2
  62.0 276.3 %reduce-scatter.2.cloned.1.call-start = ((), (), s32[]{:S(2)}) async-start(), calls=%async_computation.1 | async-start | bytes 1310720 | tf_op jit(solution)/shard_map/reduce_scatter | solution.py:202
  207.1 28.9 %copy-start.13 = (f32[512]{0:T(512)S(1)}, f32[512]{0:T(512)}, u32[]{:S(2)}) copy-start(f32[512]{0:T(512)} %param.32) | copy-start | bytes 6148
  234.6 4.2 %copy-start.1 = (f32[256,512]{1,0:T(8,128)}, f32[256,512]{1,0:T(8,128)S(1)}, u32[]{:S(2)}) copy-start(f32[256,512]{1,0:T(8,128)S(1)} %get-tuple-element.132) | copy-start | bytes 1572868
Sparse Core Ops, SparseCore 0:
  62.2 142.3 all-gather.4
  240.7 97.5 reduce-scatter.1
